TPU v7x, 256 devices: a whole 4x4x8 slice. The times are simulated.
256 devices in a mesh: ops: 128 (over y_hi, x, z, core), sec: 2 (over y_lo).
Axes of the slice: x: 4, y: 4 (y_hi: 2, y_lo: 2; y = y_hi * 2 + y_lo), z: 8, core: 2. Of those that a mesh axis runs over, the one named last changes fastest.
Arguments:
- wavefunction: bfloat16 [8, 512, 512], P('sec'), may hold values from -6 to 6
- left_ops: bfloat16 [128, 512, 512], P('ops'), may hold values from -0.25 to 0.25
- right_ops: bfloat16 [128, 512, 512], P('ops'), may hold values from -0.25 to 0.25
- shift_map: int32 [128], P('ops'), may hold values from 0 to 7
- sector_sizes: int32 [8], replicated, may hold values from 256 to 512, as said below
- step_sizes: int32 [2], replicated, may hold values from 1 to 5
- integrals: float32 [128, 3], P('ops'), may hold values from 0.25 to 1
Outputs:
- final_wave: float32 [8, 512, 512], P('sec')
- mixed_ops: bfloat16 [128, 512, 512], P('ops', None, 'sec')
Inputs may be any that keep to these rules, and one draw needn't show every extreme that they name: `sector_sizes`: each sector holds between 256 and 512 states; some sector holds exactly 512.
All inputs are finite; a program needn't handle non-finite values.
Results may differ from a plain program's by a relative error of at most 0.015.
Values may be sent and summed in bfloat16 or wider, within the bound.
A program may use at most 64 MiB of HBM per device.

v0:
```python
import math

import jax
import jax.numpy as jnp
from jax import lax
from jax.sharding import PartitionSpec as P

ITERS = 2


def broadcast(value, axis, source):
    kept = jnp.where(lax.axis_index(axis) == source, value, 0).astype(value.dtype)
    return lax.psum(kept, axis)


def padded_2(cells, sides, width):
    for axis, dim in sides:
        count = lax.axis_size(axis)
        ends = count - 1
        head = lax.slice_in_dim(cells, 0, width, axis=dim)
        tail = lax.slice_in_dim(cells, cells.shape[dim] - width, cells.shape[dim], axis=dim)
        cells = jnp.concatenate(
            [
                lax.ppermute(tail, axis, [(i, (i + 1) % count) for i in range(ends)]),
                cells,
                lax.ppermute(head, axis, [((i + 1) % count, i) for i in range(ends)]),
            ],
            axis=dim,
        )
    return cells


def shards(wavefunction, left_ops, right_ops, shift_map, sector_sizes, step_sizes, integrals):
    highest = lax.Precision.HIGHEST
    local_sec = wavefunction.shape[0]
    width = wavefunction.shape[1]
    sectors = sector_sizes.shape[0]
    count = lax.axis_size("ops") * left_ops.shape[0]
    first = lax.axis_index("sec") * local_sec
    local_sizes = lax.dynamic_slice_in_dim(sector_sizes, first, local_sec, 0)
    column = jnp.arange(width, dtype=jnp.int32)
    row_ok = (column[None, :] < local_sizes[:, None]).astype(jnp.float32)
    mask = row_ok[:, :, None] * row_ok[:, None, :]
    psi = wavefunction.astype(jnp.float32) * mask
    sources = first + jnp.arange(local_sec, dtype=jnp.int32)
    target = (sources[None, :] + shift_map[:, None]) % sectors
    routing = (jnp.arange(sectors, dtype=jnp.int32)[:, None, None] == target[None]).astype(
        jnp.float32
    )
    for step in range(ITERS):
        psi_low = psi.astype(jnp.bfloat16)
        inner = jnp.einsum(
            "kmn,snp->ksmp", left_ops, psi_low, preferred_element_type=jnp.float32
        ).astype(jnp.bfloat16)
        terms = jnp.einsum("ksmp,kqp->ksmq", inner, right_ops, preferred_element_type=jnp.float32)
        contrib = jnp.einsum("tks,ksmq->tmq", routing, terms, precision=highest)
        partial_rows = lax.psum_scatter(contrib, "ops", scatter_dimension=1, tiled=True)
        own_rows = lax.psum_scatter(
            partial_rows.astype(jnp.bfloat16), "sec", scatter_dimension=0, tiled=True
        ).astype(jnp.float32)
        hpsi = lax.all_gather(own_rows.astype(jnp.bfloat16), "ops", axis=1, tiled=True).astype(
            own_rows.dtype
        )
        factor = step_sizes[step].astype(jnp.float32) / (8.0 * math.sqrt(count))
        psi = mask * (psi - factor * hpsi)
        total = lax.psum(jnp.sum(psi * psi), "sec")
        psi = psi / jnp.sqrt(total / (sectors * width * width) + 1e-06)
    basis = broadcast(psi[0].astype(jnp.bfloat16), "sec", 0)
    col_count = width // lax.axis_size("sec")
    basis_cols = lax.dynamic_slice_in_dim(basis, lax.axis_index("sec") * col_count, col_count, 1)
    half = jnp.einsum("mp,kmn->kpn", basis, left_ops, preferred_element_type=jnp.float32).astype(
        jnp.bfloat16
    )
    rotated = (
        jnp.einsum("kpn,nq->kpq", half, basis_cols, preferred_element_type=jnp.float32) / width
    )
    padded = padded_2(rotated.astype(jnp.bfloat16), (("ops", 0),), 1).astype(rotated.dtype)
    mixed = (
        integrals[:, 0, None, None] * padded[:-2]
        + integrals[:, 1, None, None] * padded[1:-1]
        + integrals[:, 2, None, None] * padded[2:]
    )
    return (psi, mixed.astype(jnp.bfloat16))


def solution(mesh):
    placed = (
        P("sec", None, None),
        P("ops", None, None),
        P("ops", None, None),
        P("ops"),
        P(),
        P(),
        P("ops", None),
    )
    return jax.shard_map(
        shards,
        mesh=mesh,
        in_specs=placed,
        out_specs=(P("sec", None, None), P("ops", None, "sec")),
        check_vma=False,
    )
```

profile of v0, /device:TPU:1, one launch (start us, length us, event | category | flops | bytes accessed | tf_op | source)
XLA Modules:
  0.0 1710.7 jit_solution(12605415635918974398)
XLA Ops:
  7.2 0.0 copy-start
  7.2 0.0 reduce-scatter.5.cloned.1.call-start
  7.2 0.8 dynamic_slice.6
  8.0 0.1 fusion.45
  8.8 0.0 copy-done
  8.8 6.5 fusion.11
  15.3 11.7 fusion.2
  26.9 0.0 copy-start.6
  26.9 0.0 copy-start.4
  26.9 0.0 copy-start.1
  26.9 0.0 reduce-scatter.5.cloned.1.call-update
  27.0 0.0 copy-start.5
  27.0 0.0 all-gather.3.cloned.1.call-start
  27.0 0.6 copy-done.6
  27.6 0.6 dynamic-slice
  28.9 667.7 %reduce-scatter.5.cloned.1.call-done = f32[8,4,512]{2,0,1:T(8,128)} async-done(((f32[8,512,512]{2,0,1:T(8,128)}), f32[8,4,512]{2,0,1:T(8,128)}) %reduce-scatter.5.cloned.1.call-update) | async-done | bytes 65552 | tf_op jit(solution)/shard_map/reduce_scatter | solution.py:57
  696.6 0.8 convert_element_type.92
  697.4 6.4 all-reduce
  703.8 0.6 constant_dynamic-slice_fusion.1
  704.4 0.0 all-gather.3.cloned.1.call-update
  704.4 0.0 reduce-scatter.7.cloned.1.call-start
  704.5 0.0 copy-done.4
  704.5 0.6 fusion.56
  705.7 114.8 %all-gather.3.cloned.1.call-done = bf16[4,512,512]{2,0,1:T(4,128)(2,1)} async-done(((bf16[4,4,512]{2,0,1:T(4,128)(2,1)}), bf16[4,512,512]{2,0,1:T(4,128)(2,1)}) %all-gather.3.cloned.1.call-update) | async-done | bytes 2097168 | tf_op jit(solution)/shard_map/all_gather | solution.py:61
  820.5 0.0 copy-done.1
  820.5 3.8 multiply_reduce_fusion.1
  824.3 4.6 psum.21
  829.5 0.0 copy-done.5
  829.6 7.0 fusion.9
  836.5 11.7 fusion
  848.2 0.0 reduce-scatter.7.cloned.1.call-update
  848.2 0.0 all-gather.5.cloned.1.call-start
  848.3 661.5 %reduce-scatter.7.cloned.1.call-done = f32[8,4,512]{2,0,1:T(8,128)} async-done(((f32[8,512,512]{2,0,1:T(8,128)}), f32[8,4,512]{2,0,1:T(8,128)}) %reduce-scatter.7.cloned.1.call-update) | async-done | bytes 65552 | tf_op jit(solution)/shard_map/reduce_scatter | solution.py:57
  1509.8 0.8 convert_element_type.99
  1510.6 8.1 all-reduce.1
  1518.8 0.6 constant_dynamic-slice_fusion
  1519.4 0.0 all-gather.5.cloned.1.call-update
  1519.4 0.0 all-reduce.4.cloned.1.call-start
  1520.0 116.1 %all-gather.5.cloned.1.call-done = bf16[4,512,512]{2,0,1:T(4,128)(2,1)} async-done(((bf16[4,4,512]{2,0,1:T(4,128)(2,1)}), bf16[4,512,512]{2,0,1:T(4,128)(2,1)}) %all-gather.5.cloned.1.call-update) | async-done | bytes 2097168 | tf_op jit(solution)/shard_map/all_gather | solution.py:61
  1636.1 4.8 multiply_reduce_fusion
  1640.9 4.4 psum.22
  1646.0 0.0 copy-start.3
  1646.0 3.6 fusion.6
  1649.6 0.0 copy-start.2
  1649.6 2.0 copy-done.2
  1651.6 0.9 fusion.32
  1652.5 0.0 all-reduce.4.cloned.1.call-update
  1652.5 38.0 %all-reduce.4.cloned.1.call-done = bf16[512,512]{1,0:T(8,128)(2,1)} async-done(((bf16[512,512]{1,0:T(8,128)(2,1)}), bf16[512,512]{1,0:T(8,128)(2,1)}) %all-reduce.4.cloned.1.call-update) | async-done | bytes 524304 | tf_op jit(solution)/shard_map/psum | solution.py:13
  1690.5 1.8 fusion.30
  1692.4 2.6 collective-permute-start.1
  1695.0 3.1 collective-permute-start
  1698.0 0.0 copy-done.3
  1698.0 0.6 fusion.55
  1698.7 1.5 collective-permute-done.1
  1700.2 1.2 collective-permute-done
  1701.3 0.1 maximum_convert_fusion
  1701.5 2.7 fusion.34
  (1 shorter events, 0.0 us)
Async XLA Ops:
  7.2 1.6 copy-start
  7.2 689.4 %reduce-scatter.5.cloned.1.call-start = ((), (), s32[]{:S(2)}) async-start(), calls=%async_computation.2 | async-start | bytes 8454144 | tf_op jit(solution)/shard_map/reduce_scatter | solution.py:57
  26.9 0.7 copy-start.6
  26.9 677.5 %copy-start.4 = (s32[2]{0:T(128)S(1)}, s32[2]{0:T(128)}, u32[]{:S(2)}) copy-start(s32[2]{0:T(128)} %param.12) | copy-start | bytes 28
  26.9 793.6 %copy-start.1 = (bf16[4,512,512]{2,1,0:T(8,128)(2,1)S(1)}, bf16[4,512,512]{2,1,0:T(8,128)(2,1)}, u32[]{:S(2)}) copy-start(bf16[4,512,512]{2,1,0:T(8,128)(2,1)} %param.7) | copy-start | bytes 6291460
  27.0 802.6 %copy-start.5 = (bf16[1,512,512]{2,1,0:T(8,128)(2,1)S(1)}, bf16[1,512,512]{2,1,0:T(8,128)(2,1)}, u32[]{:S(2)}) copy-start(bf16[1,512,512]{2,1,0:T(8,128)(2,1)} %param.9) | copy-start | bytes 1572868
  27.0 793.5 %all-gather.3.cloned.1.call-start = ((), (), s32[]{:S(2)}) async-start(), calls=%async_computation.3 | async-start | bytes 2113536 | tf_op jit(solution)/shard_map/all_gather | solution.py:61
  704.4 805.3 %reduce-scatter.7.cloned.1.call-start = ((), (), s32[]{:S(2)}) async-start(), calls=%async_computation.4 | async-start | bytes 8454144 | tf_op jit(solution)/shard_map/reduce_scatter | solution.py:57
  848.2 787.9 %all-gather.5.cloned.1.call-start = ((), (), s32[]{:S(2)}) async-start(), calls=%async_computation.5 | async-start | bytes 2113536 | tf_op jit(solution)/shard_map/all_gather | solution.py:61
  1519.4 171.1 %all-reduce.4.cloned.1.call-start = ((), (), s32[]{:S(2)}) async-start(), calls=%async_computation.6 | async-start | bytes 1048576 | tf_op jit(solution)/shard_map/psum | solution.py:13
  1646.0 52.0 %copy-start.3 = (f32[1,3]{1,0:T(1,128)S(1)}, f32[1,3]{1,0:T(1,128)}, u32[]{:S(2)}) copy-start(f32[1,3]{1,0:T(1,128)} %param.13) | copy-start | bytes 40
  1649.6 2.0 copy-start.2
  1692.4 7.8 collective-permute-start.1
  1695.0 6.4 collective-permute-start
Sparse Core Ops, SparseCore 0:
  27.1 669.4 reduce-scatter.4
  704.5 115.9 all-gather.2
  848.3 661.3 reduce-scatter.6
  1519.5 116.5 all-gather.4
  1652.7 37.8 all-reduce.3
where the time goes:
time: 1720 us; the launch traced here: 1710 us
  waiting for transfers between devices  1600 us (93%)
  matrix products  38.6 us (2%)
  blocking collectives  23.5 us (1%)
  between operations  17.8 us (1%)
  other arithmetic  17.6 us (1%)
    reduce_scatter x2, waiting for transfers between devices, shards(): lax.psum_scatter(contrib, 'ops', scatter_dimension=1, tiled=True)  1330 us
    all_gather x2, waiting for transfers between devices, shards(): lax.all_gather(own_rows.astype(jnp.bfloat16), 'ops', axis=1, tiled=True)  231 us
    psum x1, waiting for transfers between devices, broadcast(): return lax.psum(kept, axis)  38 us
  transfers between devices with their start and end apart: 7, of which 7 were waited for; matrix products, arithmetic and copies ran while one was open for 0% of the time, Pallas kernels for 0%

commit v1 on v0

v1 whole, which is shorter than its diff:
```python
import functools
import math

import jax
import jax.numpy as jnp
from jax import lax
from jax.experimental import pallas as pl
from jax.experimental.pallas import tpu as pltpu
from jax.sharding import PartitionSpec as P

MESH = pl.DeviceIdType.MESH
F32 = jnp.float32
BF16 = jnp.bfloat16
M = 512
S = 8
OPERATORS = 128
YH, X, Z = 2, 4, 8
G = YH * X
Y = 2 * YH
XY = X * Y
OWNERS = G * Z
HALF = 2 * M
CHUNK = HALF // OWNERS
GROW = HALF // G
ZROW = HALF // Z
LAST = 3


def loop(low, high, body):
    lax.fori_loop(low, high, lambda i, c: (body(i), c)[1], 0)


def rem(a, b):
    return lax.rem(a, jnp.int32(b))


def div(a, b):
    return lax.div(a, jnp.int32(b))


def kernel(
    wave, left, right, shift, sizes, steps, integ,
    psi_out, mixed_out, scale_out,
    psi_a, psi_b, psi_f, right_t, near, lmix, chunk, acc,
    csend, cland, s1, l1, s2, l2, norm,
    pre_s, pre_r, fwd_s, fwd_r, near_s, near_r, c_s, c_r, s1_s, s1_r, s2_s, s2_r,
    ga_s, ga_r, gb_s, gb_r, gc_s, gc_r, ha_s, ha_r, hb_s, hb_r, hc_s, hc_r, n_s, n_r,
):
    ops = lax.axis_index("ops")
    sec = lax.axis_index("sec")
    core = rem(ops, 2)
    z = rem(div(ops, 2), Z)
    x = rem(div(ops, 2 * Z), X)
    yh = div(ops, 2 * Z * X)
    y = yh * 2 + sec
    g = yh * X + x
    first = sec * 4
    other = 1 - sec

    def at(xx, yy, zz, cc):
        return ((div(yy, 2) * X + xx) * Z + zz) * 2 + cc, rem(yy, 2)

    def xy_to(d):
        return rem(x + rem(d, X), X), rem(y + div(d, X), Y)

    def xy_from(d):
        return rem(x - rem(d, X) + X, X), rem(y - div(d, X) + Y, Y)

    def g_to(d):
        return rem(x + rem(d, X), X), rem(yh + div(d, X), YH)

    partner = at(x, y, z, 1 - core)
    up = at(x, rem(y + 1, Y), z, core)
    down = at(x, rem(y + Y - 1, Y), z, core)
    after = (rem(ops + 1, OPERATORS), sec)
    before = (rem(ops + OPERATORS - 1, OPERATORS), sec)

    def copy(src, dst, send, recv, device):
        return pltpu.make_async_remote_copy(
            src_ref=src, dst_ref=dst, send_sem=send, recv_sem=recv, device_id=device, device_id_type=MESH
        )

    barrier = pltpu.get_barrier_semaphore()

    def greet(device):
        pl.semaphore_signal(barrier, inc=1, device_id=device, device_id_type=MESH)

    greet(partner)
    greet(after)
    greet(before)

    def greet_xy(d):
        xx, yy = xy_to(d)
        greet(at(xx, yy, z, core))

    loop(1, XY, greet_xy)
    loop(1, Z, lambda d: greet(at(x, y, rem(z + d, Z), core)))

    row = lax.broadcasted_iota(jnp.int32, (M, 128), 0)
    col = lax.broadcasted_iota(jnp.int32, (M, 128), 1)

    def fill(t):
        size = sizes[first + t]
        for b in range(4):
            ok = (row < size) & (col < size - 128 * b)
            block = wave[t, :, 128 * b : 128 * b + 128].astype(F32)
            psi_a[sec, t, b // 2, pl.ds(b % 2 * M, M), :] = jnp.where(ok, block, 0.0).astype(BF16)

    loop(0, 4, fill)
    pl.semaphore_wait(barrier, 3 + XY - 1 + Z - 1)

    def pre(t, target, owner):
        return copy(
            psi_a.at[owner, t, core], psi_a.at[owner, t, core], pre_s.at[t], pre_r.at[t], target
        )

    for t in (0, 2, 1, 3):
        pre(t, up if t < 2 else down, sec).start()
    near_copies = [
        copy(left.at[0], near.at[0], near_s.at[0], near_r.at[0], after),
        copy(left.at[0], near.at[1], near_s.at[1], near_r.at[1], before),
    ]
    for c in near_copies:
        c.start()
    for h in range(2):
        right_t[h] = right[0, 256 * h : 256 * h + 256, :].T

    def start_chunk(t, o):
        chunk[t] = psi_a[sec, t, core, pl.ds(pl.multiple_of(o * CHUNK, CHUNK), CHUNK), :].astype(F32)

    own = [z * G + g if t == LAST else g * Z + z for t in range(4)]
    for t in range(4):
        start_chunk(t, own[t])

    def forward(t):
        ref = psi_a.at[other, t, core]
        return copy(ref, ref, fwd_s.at[t], fwd_r.at[t], partner)

    for t in (0, 2, 1, 3):
        pre(t, up, other).wait_recv()
        forward(t).start()
    for t in range(4):
        forward(t).wait_recv()

    def rows(o, n):
        return pl.ds(pl.multiple_of(o * n, n), n)

    def core_copy(it, t):
        return copy(csend.at[it, t], cland.at[it, t], c_s.at[it, t], c_r.at[it, t], partner)

    def compute(it, t, psi):
        source = rem(first + t - shift[0] + S, S)
        sa, sb = div(source, 4), rem(source, 4)
        block = jnp.concatenate(
            [psi[sa, sb, b // 2, pl.ds(b % 2 * M, M), :] for b in range(4)], axis=1
        )
        inner = jnp.dot(left[0], block, preferred_element_type=F32).astype(BF16)
        theirs = jnp.dot(inner, right_t[1 - core], preferred_element_type=F32).astype(BF16)
        csend[it, t, pl.ds(0, M), :] = theirs[:, :128]
        csend[it, t, pl.ds(M, M), :] = theirs[:, 128:]
        core_copy(it, t).start()
        mine = jnp.dot(inner, right_t[core], preferred_element_type=F32)
        acc[t, pl.ds(0, M), :] = mine[:, :128]
        acc[t, pl.ds(M, M), :] = mine[:, 128:]

    def s1_copy(it, t, d):
        if t == LAST:
            zz = rem(z + d, Z)
            device, src = at(x, y, zz, core), s1.at[it, t, rows(zz, ZROW)]
        else:
            xx, hh = g_to(d)
            device, src = at(xx, hh * 2 + sec, z, core), s1.at[it, t, rows(hh * X + xx, GROW)]
        return copy(src, l1.at[it, t, d], s1_s.at[it, t, d], s1_r.at[it, t, d], device)

    def s2_copy(it, t, d):
        if t == LAST:
            xx, hh = g_to(d)
            device, src = at(xx, hh * 2 + sec, z, core), s2.at[it, t, rows(hh * X + xx, CHUNK)]
        else:
            zz = rem(z + d, Z)
            device, src = at(x, y, zz, core), s2.at[it, t, rows(zz, CHUNK)]
        return copy(src, l2.at[it, t, d], s2_s.at[it, t, d], s2_r.at[it, t, d], device)

    def scatter(it, t):
        core_copy(it, t).wait_recv()

        def add(b):
            part = rows(b, 128)
            s1[it, t, part, :] = (acc[t, part, :] + cland[it, t, part, :].astype(F32)).astype(BF16)

        loop(0, HALF // 128, add)
        loop(1, 8, lambda d: s1_copy(it, t, d).start())

    def reduce_first(it, t):
        loop(1, 8, lambda d: s1_copy(it, t, d).wait_recv())
        total = s1[it, t, rows(z, ZROW) if t == LAST else rows(g, GROW), :].astype(F32)
        for d in range(1, 8):
            total = total + l1[it, t, d].astype(F32)
        s2[it, t] = total.astype(BF16)
        loop(1, 8, lambda d: s2_copy(it, t, d).start())

    def reduce_second(it, t, target):
        loop(1, 8, lambda d: s2_copy(it, t, d).wait_recv())
        total = s2[it, t, rows(g if t == LAST else z, CHUNK), :].astype(F32)
        for d in range(1, 8):
            total = total + l2[it, t, d].astype(F32)
        size = sizes[first + t]
        start = own[t] * CHUNK
        block = 2 * core + div(start, M)
        r = lax.broadcasted_iota(jnp.int32, (CHUNK, 128), 0) + rem(start, M)
        q = lax.broadcasted_iota(jnp.int32, (CHUNK, 128), 1) + block * 128
        factor = steps[it].astype(F32) * (1.0 / (8.0 * math.sqrt(OPERATORS)))
        value = jnp.where((r < size) & (q < size), chunk[t] - factor * total, 0.0)
        chunk[t] = value
        target[sec, t, core, rows(own[t], CHUNK), :] = value.astype(BF16)

    def step(it, psi, target):
        compute(it, 0, psi)
        compute(it, 1, psi)
        scatter(it, 0)
        compute(it, 2, psi)
        scatter(it, 1)
        compute(it, 3, psi)
        scatter(it, 2)
        scatter(it, 3)
        for t in range(4):
            reduce_first(it, t)
        for t in range(4):
            reduce_second(it, t, target)

    def same(ref, send, recv, device):
        return copy(ref, ref, send, recv, device)

    step(0, psi_a, psi_b)

    def ga(d):
        ref = psi_b.at[sec, pl.ds(0, 3), core, rows(own[0], CHUNK)]
        return same(ref, ga_s.at[0, d], ga_r.at[0, d], at(x, y, rem(z + d, Z), core))

    def gb(d):
        xx, yy = xy_to(d)
        ref = psi_b.at[sec, pl.ds(0, 3), core, rows(g, GROW)]
        return same(ref, gb_s.at[0, d], gb_r.at[0, d], at(xx, yy, z, core))

    def gc(d):
        xx, yy = xy_from(d)
        ref = psi_b.at[rem(yy, 2), pl.ds(0, 3), core, rows(div(yy, 2) * X + xx, GROW)]
        return same(ref, gc_s.at[0, d], gc_r.at[0, d], partner)

    def ha(d):
        xx, yy = xy_to(d)
        ref = psi_b.at[sec, LAST, core, rows(own[LAST], CHUNK)]
        return same(ref, ha_s.at[0, d], ha_r.at[0, d], at(xx, yy, z, core))

    def hb(d):
        ref = psi_b.at[pl.ds(0, 2), LAST, core, rows(z, ZROW)]
        return same(ref, hb_s.at[0, d], hb_r.at[0, d], at(x, y, rem(z + d, Z), core))

    def hc(d):
        ref = psi_b.at[pl.ds(0, 2), LAST, core, rows(rem(z - d + Z, Z), ZROW)]
        return same(ref, hc_s.at[0, d], hc_r.at[0, d], partner)

    loop(1, Z, lambda d: ga(d).start())
    loop(1, XY, lambda d: ha(d).start())
    loop(1, Z, lambda d: ga(d).wait_recv())
    loop(1, XY, lambda d: gb(d).start())
    loop(1, XY, lambda d: ha(d).wait_recv())
    loop(1, Z, lambda d: hb(d).start())
    gc(0).start()
    hc(0).start()

    def pass_g(d):
        gb(d).wait_recv()
        gc(d).start()

    def pass_h(d):
        hb(d).wait_recv()
        hc(d).start()

    loop(1, XY, pass_g)
    loop(1, Z, pass_h)
    loop(0, XY, lambda d: gc(d).wait_recv())
    loop(0, Z, lambda d: hc(d).wait_recv())

    def squares(ref, a, t):
        def add(i, total):
            part = ref[a, t, div(i, 8), rows(rem(i, 8), 128), :].astype(F32)
            return total + jnp.sum((part * part).reshape(16, 8, 128), axis=0)

        return lax.fori_loop(0, 16, add, jnp.zeros((8, 128), F32))

    step(1, psi_b, psi_f)

    def ia(d):
        ref = psi_f.at[sec, pl.ds(0, 3), core, rows(own[0], CHUNK)]
        return same(ref, ga_s.at[1, d], ga_r.at[1, d], at(x, y, rem(z + d, Z), core))

    def ib(d):
        xx, hh = g_to(d)
        ref = psi_f.at[sec, pl.ds(0, 3), core, rows(g, GROW)]
        return same(ref, gb_s.at[1, d], gb_r.at[1, d], at(xx, hh * 2 + sec, z, core))

    def ic(d):
        gg = rem(yh - div(d, X) + YH, YH) * X + rem(x - rem(d, X) + X, X)
        ref = psi_f.at[sec, pl.ds(0, 3), core, rows(gg, GROW)]
        return same(ref, gc_s.at[1, d], gc_r.at[1, d], partner)

    def ja(d):
        xx, hh = g_to(d)
        ref = psi_f.at[sec, LAST, core, rows(own[LAST], CHUNK)]
        return same(ref, ha_s.at[1, d], ha_r.at[1, d], at(xx, hh * 2 + sec, z, core))

    def jb(d):
        ref = psi_f.at[sec, LAST, core, rows(z, ZROW)]
        return same(ref, hb_s.at[1, d], hb_r.at[1, d], at(x, y, rem(z + d, Z), core))

    def jc(d):
        ref = psi_f.at[sec, LAST, core, rows(rem(z - d + Z, Z), ZROW)]
        return same(ref, hc_s.at[1, d], hc_r.at[1, d], partner)

    def basis_to(d):
        xx, hh = g_to(d)
        ref = psi_f.at[0, 0, core, rows(g, GROW)]
        return same(ref, gb_s.at[1, 8 + d], gb_r.at[1, 8 + d], at(xx, hh * 2 + other, z, core))

    def basis_pass(d):
        gg = rem(yh - div(d, X) + YH, YH) * X + rem(x - rem(d, X) + X, X)
        ref = psi_f.at[0, 0, core, rows(gg, GROW)]
        return same(ref, gc_s.at[1, 8 + d], gc_r.at[1, 8 + d], partner)

    loop(1, Z, lambda d: ia(d).start())
    loop(1, G, lambda d: ja(d).start())
    loop(1, Z, lambda d: ia(d).wait_recv())

    @pl.when(sec == 0)
    def _():
        loop(0, G, lambda d: basis_to(d).start())

    loop(1, G, lambda d: ib(d).start())
    loop(1, G, lambda d: ja(d).wait_recv())
    loop(1, Z, lambda d: jb(d).start())
    ic(0).start()
    jc(0).start()

    for c in near_copies:
        c.wait_recv()
    w0 = jnp.where(ops == 0, 0.0, integ[0, 0])
    w1 = integ[0, 1]
    w2 = jnp.where(ops == OPERATORS - 1, 0.0, integ[0, 2])

    def mix(i):
        part = rows(i, 64)
        lmix[part, :] = (
            w0 * near[0, part, :].astype(F32)
            + w1 * left[0, part, :].astype(F32)
            + w2 * near[1, part, :].astype(F32)
        ).astype(BF16)

    loop(0, M // 64, mix)

    total1 = jnp.zeros((8, 128), F32)
    for a in range(2):
        for t in range(4):
            total1 = total1 + squares(psi_b, a, t)

    @pl.when(sec == 1)
    def _():
        def pass_basis(d):
            basis_to(d).wait_recv()
            basis_pass(d).start()

        loop(0, G, pass_basis)

    def pass_i(d):
        ib(d).wait_recv()
        ic(d).start()

    def pass_j(d):
        jb(d).wait_recv()
        jc(d).start()

    loop(1, G, pass_i)
    loop(1, Z, pass_j)

    @pl.when(sec == 1)
    def _():
        loop(0, G, lambda d: basis_pass(d).wait_recv())

    loop(0, G, lambda d: ic(d).wait_recv())
    loop(0, Z, lambda d: jc(d).wait_recv())

    total2 = jnp.zeros((8, 128), F32)
    for t in range(4):
        total2 = total2 + squares(psi_f, sec, t)
    norm[0] = total2
    exchange = copy(norm.at[0], norm.at[1], n_s.at[0], n_r.at[0], at(x, 2 * yh + other, z, core))
    exchange.start()

    psi_out[...] = psi_f[sec]
    basis = jnp.concatenate([psi_f[0, 0, b // 2, pl.ds(b % 2 * M, M), :] for b in range(4)], axis=1)
    basis_cols = jnp.concatenate([psi_f[0, 0, sec, pl.ds(b * M, M), :] for b in range(2)], axis=1)
    half = jnp.dot(lmix[...], basis_cols, preferred_element_type=F32).astype(BF16)
    rotated = lax.dot_general(
        basis, half, (((0,), (0,)), ((), ())), preferred_element_type=F32
    )

    exchange.wait_recv()
    count = float(S * M * M)
    sum1 = jnp.sum(total1, axis=(0, 1), keepdims=True)
    sum2 = jnp.sum(norm[0] + norm[1], axis=(0, 1), keepdims=True)
    square = sum2 * (1.0 / count) + 1e-06 * (sum1 * (1.0 / count) + 1e-06)
    scale = lax.rsqrt(square)
    scale_out[...] = jnp.broadcast_to(scale, (8, 128))
    mixed_out[0] = (rotated * (scale * scale * (1.0 / M))).astype(BF16)

    exchange.wait_send()
    for c in near_copies:
        c.wait_send()
    for t in range(4):
        pre(t, up, sec).wait_send()
        forward(t).wait_send()
    for it in range(2):
        for t in range(4):
            core_copy(it, t).wait_send()
            loop(1, 8, lambda d, it=it, t=t: s1_copy(it, t, d).wait_send())
            loop(1, 8, lambda d, it=it, t=t: s2_copy(it, t, d).wait_send())
    loop(1, Z, lambda d: ga(d).wait_send())
    loop(1, XY, lambda d: gb(d).wait_send())
    loop(0, XY, lambda d: gc(d).wait_send())
    loop(1, XY, lambda d: ha(d).wait_send())
    loop(1, Z, lambda d: hb(d).wait_send())
    loop(0, Z, lambda d: hc(d).wait_send())
    loop(1, Z, lambda d: ia(d).wait_send())
    loop(1, G, lambda d: ib(d).wait_send())
    loop(0, G, lambda d: ic(d).wait_send())
    loop(1, G, lambda d: ja(d).wait_send())
    loop(1, Z, lambda d: jb(d).wait_send())
    loop(0, Z, lambda d: jc(d).wait_send())

    @pl.when(sec == 0)
    def _():
        loop(0, G, lambda d: basis_to(d).wait_send())

    @pl.when(sec == 1)
    def _():
        loop(0, G, lambda d: basis_pass(d).wait_send())


def shards(*args):
    vmem = pl.BlockSpec(memory_space=pltpu.VMEM)
    smem = pl.BlockSpec(memory_space=pltpu.SMEM)
    dma = pltpu.SemaphoreType.DMA
    psi = pltpu.VMEM((2, 4, 2, HALF, 128), BF16)
    raw, mixed, scale = pl.pallas_call(
        kernel,
        out_shape=(
            jax.ShapeDtypeStruct((4, 2, HALF, 128), BF16),
            jax.ShapeDtypeStruct((1, M, M // 2), BF16),
            jax.ShapeDtypeStruct((8, 128), F32),
        ),
        in_specs=[vmem, vmem, vmem, smem, smem, smem, smem],
        out_specs=(vmem, vmem, vmem),
        scratch_shapes=[
            psi,
            psi,
            psi,
            pltpu.VMEM((2, M, 256), BF16),
            pltpu.VMEM((2, M, M), BF16),
            pltpu.VMEM((M, M), BF16),
            pltpu.VMEM((4, CHUNK, 128), F32),
            pltpu.VMEM((4, HALF, 128), F32),
            pltpu.VMEM((2, 4, HALF, 128), BF16),
            pltpu.VMEM((2, 4, HALF, 128), BF16),
            pltpu.VMEM((2, 4, HALF, 128), BF16),
            pltpu.VMEM((2, 4, 8, GROW, 128), BF16),
            pltpu.VMEM((2, 4, GROW, 128), BF16),
            pltpu.VMEM((2, 4, 8, CHUNK, 128), BF16),
            pltpu.VMEM((2, 8, 128), F32),
            dma((4,)), dma((4,)), dma((4,)), dma((4,)), dma((2,)), dma((2,)),
            dma((2, 4)), dma((2, 4)), dma((2, 4, 8)), dma((2, 4, 8)), dma((2, 4, 8)), dma((2, 4, 8)),
            dma((2, Z)), dma((2, Z)), dma((2, XY)), dma((2, XY)), dma((2, XY)), dma((2, XY)),
            dma((2, XY)), dma((2, XY)), dma((2, Z)), dma((2, Z)), dma((2, Z)), dma((2, Z)),
            dma((1,)), dma((1,)),
        ],
        compiler_params=pltpu.CompilerParams(
            collective_id=0, has_side_effects=True, vmem_limit_bytes=60 * 2**20
        ),
        name="dmrg_window",
    )(*args)
    wave = raw.reshape(4, 4, M, 128).transpose(0, 2, 1, 3).reshape(4, M, M)
    return wave.astype(F32) * scale[0, 0], mixed


def solution(mesh):
    placed = (
        P("sec", None, None),
        P("ops", None, None),
        P("ops", None, None),
        P("ops"),
        P(),
        P(),
        P("ops", None),
    )
    return jax.shard_map(
        shards,
        mesh=mesh,
        in_specs=placed,
        out_specs=(P("sec", None, None), P("ops", None, "sec")),
        check_vma=False,
    )
```

time: 1720 us -> 139 us (0.08)
  waiting for transfers between devices: 1600 us -> 0 us
  Pallas kernels: 0 us -> 130 us
  matrix products: 38.6 us -> 0 us
  blocking collectives: 23.5 us -> 0 us
    reduce_scatter x2 -> x0, waiting for transfers between devices: 1330 us -> none  [shards(): lax.psum_scatter(contrib, 'ops', scatter_dimension=1, tiled=True)]
    all_gather x2 -> x0, waiting for transfers between devices: 231 us -> none  [shards(): lax.all_gather(own_rows.astype(jnp.bfloat16), 'ops', axis=1, tiled=True)]
    pallas_call x0 -> x1, Pallas kernels: none -> 130 us  [shards(): pl.pallas_call(kernel, out_shape=(jax.ShapeDtypeStruct((4, 2, HALF, 128),...]
    dot_general x5 -> x0, matrix products: 38.6 us -> none  [the longest x2 23.4 us: shards(): contrib = jnp.einsum('tks,ksmq->tmq', routing, terms, precision=highest)]
    psum x1 -> x0, waiting for transfers between devices: 38 us -> none  [broadcast(): return lax.psum(kept, axis)]
  transfers between devices with their start and end apart: 7 -> 0, of which waited for: 7 -> 0; matrix products, arithmetic and copies ran while one was open for 0% -> 0% of each run, Pallas kernels for 0% -> 0%
where the time goes in v1:
time: 139 us; the launch traced here: 138 us
  Pallas kernels  130 us (94%)
  local copies, waits for them, and re-layouts  4.51 us (3%)
  other arithmetic  2.52 us (2%)
    pallas_call x1, Pallas kernels, shards(): pl.pallas_call(kernel, out_shape=(jax.ShapeDtypeStruct((4, 2, HALF, 128),...  130 us

profile of v1, /device:TPU:1, one launch (start us, length us, event | category | flops | bytes accessed | tf_op | source)
XLA Modules:
  0.0 138.3 jit_solution(2718501943378814716)
XLA Ops:
  1.3 130.0 %dmrg_window.1 = (bf16[4,2,1024,128]{3,2,1,0:T(8,128)(2,1)}, bf16[1,512,256]{2,1,0:T(8,128)(2,1)}, f32[8,128]{1,0:T(8,128)}) custom-call(bf16[4,512,512]{2,1,0:T(8,128)(2,1)} %wave.1, bf16[1,512,512]{2,1,0:T(8,128)(2,1)} %left.1, bf16[1,512,512]{2,1,0:T(8,128)(2,1)} %right.1, s32[1]{0:T(128)S(6)} %copy.14.shift, s32[8]{0:T(128)} %sizes.1, s32[2]{0:T(128)} %steps.1, ...), custom_call_target="tpu_custom_call" | custom-call | tf_op jit(solution)/shard_map/dmrg_window/pallas_call | solution.py:454
  131.3 1.2 slice.3
  132.5 2.5 %convert_multiply_fusion = f32[4,2,1024,128]{3,2,1,0:T(8,128)S(1)} fusion(bf16[4,2,1024,128]{3,2,1,0:T(8,128)(2,1)} %get-tuple-element.5, f32[]{:T(128)} %bitcast), kind=kLoop, calls=%fused_computation.1 | loop fusion | flops 2097152 | bytes 6291460 | tf_op jit(solution)/shard_map/mul | solution.py:491
  135.0 0.0 copy-start
  135.0 2.6 %copy.12 = f32[4,4,64,8,128]{4,3,1,2,0:T(8,128)} copy(f32[4,4,64,8,128]{4,3,2,1,0:T(8,128)S(1)} %bitcast.8) | data formatting | bytes 8388608 | tf_op jit(solution)/shard_map/mul | solution.py:491
  137.6 0.0 copy-done
  137.6 0.7 copy.15
Async XLA Ops:
  135.0 2.6 %copy-start = (bf16[1,512,256]{2,1,0:T(8,128)(2,1)S(1)}, bf16[1,512,256]{2,1,0:T(8,128)(2,1)}, u32[]{:S(2)}) copy-start(bf16[1,512,256]{2,1,0:T(8,128)(2,1)} %get-tuple-element.11) | copy-start | bytes 786436

commit v2 on v0

v2 whole, which is shorter than its diff:
```python
import math

import jax
import jax.numpy as jnp
from jax import lax
from jax.experimental import pallas as pl
from jax.experimental.pallas import tpu as pltpu
from jax.sharding import PartitionSpec as P

MESH = pl.DeviceIdType.MESH
F32 = jnp.float32
BF16 = jnp.bfloat16
M = 512
S = 8
OPERATORS = 128
YH, X, Z = 2, 4, 8
G = YH * X
Y = 2 * YH
XY = X * Y
HALF = 2 * M
CHUNK = HALF // (G * Z)
BLOCK = HALF // 8
LAST = 3
ORDER = (3, 0, 1, 2)


def loop(low, high, body):
    lax.fori_loop(low, high, lambda i, c: (body(i), c)[1], 0)


def rem(a, b):
    return lax.rem(a, jnp.int32(b))


def div(a, b):
    return lax.div(a, jnp.int32(b))


def rows(o, n):
    return pl.ds(pl.multiple_of(o * n, n), n)


def kernel(
    wave, left, right, shift, sizes, steps, integ,
    psi_out, mixed_out, scale_out,
    psi, bas, right_t, near, lmix, chunk, give, acc,
    csend, cland, s1, l1, l1z, s2, s2z, l2, l2z, nz, nxy, nc, total, rotated,
    near_s, near_r, c_s, c_r, s1_s, s1_r, s2_s, s2_r, a_s, a_r, b_s, b_r, f_s, f_r, bas_s, bas_r, n_s, n_r,
):
    ops = lax.axis_index("ops")
    sec = lax.axis_index("sec")
    core = rem(ops, 2)
    z = rem(div(ops, 2), Z)
    x = rem(div(ops, 2 * Z), X)
    yh = div(ops, 2 * Z * X)
    y = yh * 2 + sec
    g = yh * X + x
    first = sec * 4

    def at(xx, yy, zz, cc):
        return ((div(yy, 2) * X + xx) * Z + zz) * 2 + cc, rem(yy, 2)

    def xy_to(d):
        return rem(x + rem(d, X), X), rem(y + div(d, X), Y)

    def g_to(d):
        return rem(x + rem(d, X), X), rem(y + 2 * div(d, X), Y)

    partner = at(x, y, z, 1 - core)
    after = (rem(ops + 1, OPERATORS), sec)
    before = (rem(ops + OPERATORS - 1, OPERATORS), sec)

    def copy(src, dst, send, recv, device):
        return pltpu.make_async_remote_copy(
            src_ref=src, dst_ref=dst, send_sem=send, recv_sem=recv, device_id=device, device_id_type=MESH
        )

    sent = []

    def start(made):
        made.start()
        sent.append(made.wait_send)

    def group(low, high, make, whole, send, recv):
        loop(low, high, lambda d: make(d).start())
        sent.append(copy(whole, whole, send, recv, partner).wait_send)

    def arrived(whole, send, recv):
        copy(whole, whole, send, recv, partner).wait_recv()

    barrier = pltpu.get_barrier_semaphore()

    def greet(device):
        pl.semaphore_signal(barrier, inc=1, device_id=device, device_id_type=MESH)

    greet(after)
    greet(before)

    def greet_xy(d):
        xx, yy = xy_to(d)
        greet(at(xx, yy, z, core))

    loop(1, XY, greet_xy)
    loop(1, Z, lambda d: greet(at(x, y, rem(z + d, Z), core)))
    greet(partner)

    row = lax.broadcasted_iota(jnp.int32, (M, 128), 0)
    col = lax.broadcasted_iota(jnp.int32, (M, 128), 1)

    def fill(t):
        size = sizes[first + t]
        for b in range(4):
            ok = (row < size) & (col < size - 128 * b)
            block = wave[t, :, 128 * b : 128 * b + 128].astype(F32)
            psi[0, t, b // 2, pl.ds(b % 2 * M, M), :] = jnp.where(ok, block, 0.0).astype(BF16)

    loop(0, 4, fill)
    for h in range(2):
        right_t[h] = right[0, 256 * h : 256 * h + 256, :].T
    own = [z * G + g if t == LAST else g * Z + z for t in range(4)]
    for t in range(4):
        chunk[t] = psi[0, t, core, rows(own[t], CHUNK), :].astype(F32)

    def columns(ref):
        return jnp.concatenate([ref[b // 2, pl.ds(b % 2 * M, M), :] for b in range(4)], axis=1)

    def compute(it, s):
        inner = jnp.dot(left[0], columns(psi.at[it, s]), preferred_element_type=F32).astype(BF16)
        theirs = jnp.dot(inner, right_t[1 - core], preferred_element_type=F32).astype(BF16)
        give[s, pl.ds(0, M), :] = theirs[:, :128]
        give[s, pl.ds(M, M), :] = theirs[:, 128:]
        mine = jnp.dot(inner, right_t[core], preferred_element_type=F32)
        acc[s, pl.ds(0, M), :] = mine[:, :128]
        acc[s, pl.ds(M, M), :] = mine[:, 128:]

    def source(a, t):
        s = rem(a * 4 + t - first - shift[0] + 2 * S, S)
        return jnp.minimum(s, 3), jnp.where(s < 4, 1.0, 0.0).astype(F32)

    def core_copy(it, t):
        return copy(csend.at[it, t], cland.at[it, t], c_s.at[it, t], c_r.at[it, t], partner)

    def pick(it, t):
        for a in range(2):
            s, gate = source(a, t)
            for b in range(4):
                part = pl.ds(256 * b, 256)
                csend[it, t, a, part, :] = (give[s, part, :].astype(F32) * gate).astype(BF16)

    def scatter(it, t):
        core_copy(it, t).wait_recv()
        for a in range(2):
            s, gate = source(a, t)
            for b in range(4):
                part = pl.ds(256 * b, 256)
                s1[it, t, a, part, :] = (
                    acc[s, part, :] * gate + cland[it, t, a, part, :].astype(F32)
                ).astype(BF16)
        sems = s1_s.at[it, t], s1_r.at[it, t]
        if t == LAST:

            def make(d):
                zz = rem(z + d, Z)
                return copy(s1.at[it, t, :, rows(zz, BLOCK)], l1z.at[it, d], *sems, at(x, y, zz, core))

            group(1, Z, make, l1z.at[it, pl.ds(1, Z - 1)], *sems)
        else:

            def make(d):
                xx, yy = xy_to(d)
                src = s1.at[it, t, rem(yy, 2), rows(div(yy, 2) * X + xx, BLOCK)]
                return copy(src, l1.at[it, t, d], *sems, at(xx, yy, z, core))

            group(1, XY, make, l1.at[it, t, pl.ds(1, XY - 1)], *sems)

    def reduce_first(it, t):
        sems = s1_s.at[it, t], s1_r.at[it, t]
        send = s2_s.at[it, t], s2_r.at[it, t]
        if t == LAST:
            arrived(l1z.at[it, pl.ds(1, Z - 1)], *sems)
            for a in range(2):
                value = s1[it, t, a, rows(z, BLOCK), :].astype(F32)
                for d in range(1, Z):
                    value = value + l1z[it, d, a].astype(F32)
                s2z[it, a] = value.astype(BF16)

            def make(d):
                xx, yy = xy_to(d)
                src = s2z.at[it, rem(yy, 2), rows(div(yy, 2) * X + xx, CHUNK)]
                return copy(src, l2z.at[it, d], *send, at(xx, yy, z, core))

            group(1, XY, make, l2z.at[it, pl.ds(1, XY - 1)], *send)
        else:
            arrived(l1.at[it, t, pl.ds(1, XY - 1)], *sems)
            value = s1[it, t, sec, rows(g, BLOCK), :].astype(F32)
            for d in range(1, XY):
                value = value + l1[it, t, d].astype(F32)
            s2[it, t] = value.astype(BF16)

            def make(d):
                zz = rem(z + d, Z)
                return copy(s2.at[it, t, rows(zz, CHUNK)], l2.at[it, t, d], *send, at(x, y, zz, core))

            group(1, Z, make, l2.at[it, t, pl.ds(1, Z - 1)], *send)

    def z_copies(ref, sems):
        return lambda d: copy(ref, ref, *sems, at(x, y, rem(z + d, Z), core))

    def g_copies(ref, sems):
        def make(d):
            xx, yy = g_to(d)
            return copy(ref, ref, *sems, at(xx, yy, z, core))

        return make

    def reduce_second(it, t):
        sems = s2_s.at[it, t], s2_r.at[it, t]
        if t == LAST:
            arrived(l2z.at[it, pl.ds(1, XY - 1)], *sems)
            value = s2z[it, sec, rows(g, CHUNK), :].astype(F32)
            for d in range(1, XY):
                value = value + l2z[it, d].astype(F32)
        else:
            arrived(l2.at[it, t, pl.ds(1, Z - 1)], *sems)
            value = s2[it, t, rows(z, CHUNK), :].astype(F32)
            for d in range(1, Z):
                value = value + l2[it, t, d].astype(F32)
        size = sizes[first + t]
        begin = own[t] * CHUNK
        r = lax.broadcasted_iota(jnp.int32, (CHUNK, 128), 0) + rem(begin, M)
        q = lax.broadcasted_iota(jnp.int32, (CHUNK, 128), 1) + (2 * core + div(begin, M)) * 128
        factor = steps[it].astype(F32) * (1.0 / (8.0 * math.sqrt(OPERATORS)))
        value = jnp.where((r < size) & (q < size), chunk[t] - factor * value, 0.0)
        chunk[t] = value
        psi[it + 1, t, core, rows(own[t], CHUNK), :] = value.astype(BF16)
        ref = psi.at[it + 1, t, core, rows(own[t], CHUNK)]
        send = a_s.at[it, t], a_r.at[it, t]
        whole = psi.at[it + 1, t, core, pl.ds(0, 7 * CHUNK)]
        group(1, 8, (g_copies if t == LAST else z_copies)(ref, send), whole, *send)

    def gather_second(it, t):
        arrived(psi.at[it + 1, t, core, pl.ds(0, 7 * CHUNK)], a_s.at[it, t], a_r.at[it, t])
        ref = psi.at[it + 1, t, core, rows(z if t == LAST else g, BLOCK)]
        send = b_s.at[it, t], b_r.at[it, t]
        if it == 1 and t == 0:
            src = psi.at[2, 0, core, rows(g, BLOCK)]
            dst = bas.at[core, rows(g, BLOCK)]

            def make(d):
                xx, yy = xy_to(rem(d, X) + X * (2 * div(d, X) + 1))
                return copy(src, dst, bas_s.at[0], bas_r.at[0], at(xx, yy, z, core))

            @pl.when(sec == 0)
            def _():
                loop(0, G, lambda d: make(d).start())

            @sent.append
            def _():
                @pl.when(sec == 0)
                def _():
                    copy(bas.at[0], bas.at[0], bas_s.at[0], bas_r.at[0], partner).wait_send()

        whole = psi.at[it + 1, t, core, pl.ds(0, 7 * BLOCK)]
        group(1, 8, (z_copies if t == LAST else g_copies)(ref, send), whole, *send)

    def forward_copy(it, t):
        ref = psi.at[it + 1, t, core]
        return copy(ref, ref, f_s.at[it, t], f_r.at[it, t], partner)

    def forward(it, t):
        arrived(psi.at[it + 1, t, core, pl.ds(0, 7 * BLOCK)], b_s.at[it, t], b_r.at[it, t])
        start(forward_copy(it, t))

    def norm_z(it):
        value = jnp.zeros((8, 128), F32)
        for t in range(4):
            part = chunk[t]
            value = value + jnp.sum((part * part).reshape(CHUNK // 8, 8, 128), axis=0)
        nz[it, 0] = value
        sems = n_s.at[it, 0], n_r.at[it, 0]

        def make(d):
            return copy(nz.at[it, 0], nz.at[it, d], *sems, at(x, y, rem(z + d, Z), core))

        group(1, Z, make, nz.at[it, pl.ds(1, Z - 1)], *sems)

    def norm_xy(it):
        arrived(nz.at[it, pl.ds(1, Z - 1)], n_s.at[it, 0], n_r.at[it, 0])
        nxy[it, 0] = jnp.sum(nz[it], axis=0)
        sems = n_s.at[it, 1], n_r.at[it, 1]

        def make(d):
            xx, yy = xy_to(d)
            return copy(nxy.at[it, 0], nxy.at[it, d], *sems, at(xx, yy, z, core))

        group(1, XY, make, nxy.at[it, pl.ds(1, XY - 1)], *sems)

    def norm_copy(it):
        return copy(nc.at[it, 0], nc.at[it, 1], n_s.at[it, 2], n_r.at[it, 2], partner)

    def norm_core(it):
        arrived(nxy.at[it, pl.ds(1, XY - 1)], n_s.at[it, 1], n_r.at[it, 1])
        nc[it, 0] = jnp.sum(nxy[it], axis=0)
        start(norm_copy(it))

    def norm_end(it):
        norm_copy(it).wait_recv()
        total[it] = nc[it, 0] + nc[it, 1]

    near_copies = [
        copy(left.at[0], near.at[0], near_s.at[0], near_r.at[0], after),
        copy(left.at[0], near.at[1], near_s.at[1], near_r.at[1], before),
    ]

    def mix():
        for c in near_copies:
            c.wait_recv()
        w0 = jnp.where(ops == 0, 0.0, integ[0, 0])
        w1 = integ[0, 1]
        w2 = jnp.where(ops == OPERATORS - 1, 0.0, integ[0, 2])

        def body(i):
            part = rows(i, 64)
            lmix[part, :] = (
                w0 * near[0, part, :].astype(F32)
                + w1 * left[0, part, :].astype(F32)
                + w2 * near[1, part, :].astype(F32)
            ).astype(BF16)

        loop(0, M // 64, body)

    def write_wave(t):
        for b in range(4):
            psi_out[t, :, 128 * b : 128 * b + 128] = psi[2, t, b // 2, pl.ds(b % 2 * M, M), :]

    bas_copy = copy(bas.at[core], bas.at[core], bas_s.at[1], bas_r.at[1], partner)

    def basis_forward():
        @pl.when(sec == 1)
        def _():
            arrived(bas.at[core], bas_s.at[0], bas_r.at[0])
            bas_copy.start()

        @sent.append
        def _():
            @pl.when(sec == 1)
            def _():
                bas_copy.wait_send()

    def rotate():
        @pl.when(sec == 0)
        def _():
            bas[...] = psi[2, 0]

        @pl.when(sec == 1)
        def _():
            bas_copy.wait_recv()

        basis_cols = jnp.concatenate([bas[sec, pl.ds(b * M, M), :] for b in range(2)], axis=1)
        half = jnp.dot(lmix[...], basis_cols, preferred_element_type=F32).astype(BF16)
        rotated[...] = lax.dot_general(
            columns(bas), half, (((0,), (0,)), ((), ())), preferred_element_type=F32
        )

    for s in range(4):
        compute(0, s)
    for it in range(2):
        for t in ORDER:
            pick(it, t)
            if it == 0 and t == ORDER[0]:
                pl.semaphore_wait(barrier, 3 + XY - 1 + Z - 1)
            start(core_copy(it, t))
        for t in ORDER:
            scatter(it, t)
            if it == 0 and t == LAST:
                for c in near_copies:
                    start(c)
        if it == 1:
            mix()
        reduce_first(it, 0)
        reduce_first(it, 3)
        reduce_first(it, 1)
        reduce_second(it, 0)
        reduce_first(it, 2)
        reduce_second(it, 3)
        reduce_second(it, 1)
        gather_second(it, 0)
        reduce_second(it, 2)
        norm_z(it)
        gather_second(it, 1)
        gather_second(it, 3)
        forward(it, 0)
        if it == 1:
            basis_forward()
        gather_second(it, 2)
        norm_xy(it)
        forward(it, 1)
        forward(it, 3)
        forward_copy(it, 0).wait_recv()
        if it == 0:
            compute(1, 0)
        else:
            write_wave(0)
            rotate()
        forward_copy(it, 1).wait_recv()
        if it == 0:
            compute(1, 1)
        else:
            write_wave(1)
        forward(it, 2)
        norm_core(it)
        for t in (3, 2):
            forward_copy(it, t).wait_recv()
            if it == 0:
                compute(1, t)
            else:
                write_wave(t)
        norm_end(it)

    count = float(S * M * M)
    sum1 = jnp.sum(total[0], axis=(0, 1), keepdims=True)
    sum2 = jnp.sum(total[1], axis=(0, 1), keepdims=True)
    square = sum2 * (1.0 / count) + 1e-06 * (sum1 * (1.0 / count) + 1e-06)
    scale = lax.rsqrt(square)
    scale_out[...] = jnp.broadcast_to(scale, (1, M))
    mixed_out[0] = (rotated[...] * (scale * scale * (1.0 / M))).astype(BF16)

    for wait in sent:
        wait()


def shards(*args):
    vmem = pl.BlockSpec(memory_space=pltpu.VMEM)
    smem = pl.BlockSpec(memory_space=pltpu.SMEM)

    def low(*shape):
        return pltpu.VMEM(shape, BF16)

    def full(*shape):
        return pltpu.VMEM(shape, F32)

    def pair(*shape):
        return [pltpu.SemaphoreType.DMA(shape)] * 2

    wave, mixed, scale = pl.pallas_call(
        kernel,
        out_shape=(
            jax.ShapeDtypeStruct((4, M, M), BF16),
            jax.ShapeDtypeStruct((1, M, M // 2), BF16),
            jax.ShapeDtypeStruct((1, M), F32),
        ),
        in_specs=[vmem, vmem, vmem, smem, smem, smem, smem],
        out_specs=(vmem, vmem, vmem),
        scratch_shapes=[
            low(3, 4, 2, HALF, 128),
            low(2, HALF, 128),
            low(2, M, 256),
            low(2, M, M),
            low(M, M),
            full(4, CHUNK, 128),
            low(4, HALF, 128),
            full(4, HALF, 128),
            low(2, 4, 2, HALF, 128),
            low(2, 4, 2, HALF, 128),
            low(2, 4, 2, HALF, 128),
            low(2, 3, XY, BLOCK, 128),
            low(2, Z, 2, BLOCK, 128),
            low(2, 3, BLOCK, 128),
            low(2, 2, BLOCK, 128),
            low(2, 3, Z, CHUNK, 128),
            low(2, XY, CHUNK, 128),
            full(2, Z, 8, 128),
            full(2, XY, 8, 128),
            full(2, 2, 8, 128),
            full(2, 8, 128),
            full(M, M // 2),
            *pair(2),
            *pair(2, 4),
            *pair(2, 4),
            *pair(2, 4),
            *pair(2, 4),
            *pair(2, 4),
            *pair(2, 4),
            *pair(2),
            *pair(2, 3),
        ],
        compiler_params=pltpu.CompilerParams(
            collective_id=0, has_side_effects=True, vmem_limit_bytes=60 * 2**20
        ),
        name="dmrg_window",
    )(*args)
    return wave.astype(F32) * scale, mixed


def solution(mesh):
    placed = (
        P("sec", None, None),
        P("ops", None, None),
        P("ops", None, None),
        P("ops"),
        P(),
        P(),
        P("ops", None),
    )
    return jax.shard_map(
        shards,
        mesh=mesh,
        in_specs=placed,
        out_specs=(P("sec", None, None), P("ops", None, "sec")),
        check_vma=False,
    )
```

time: 1720 us -> 113 us (0.07)
  waiting for transfers between devices: 1600 us -> 0 us
  Pallas kernels: 0 us -> 106 us
  matrix products: 38.6 us -> 0 us
  blocking collectives: 23.5 us -> 0 us
    reduce_scatter x2 -> x0, waiting for transfers between devices: 1330 us -> none  [shards(): lax.psum_scatter(contrib, 'ops', scatter_dimension=1, tiled=True)]
    all_gather x2 -> x0, waiting for transfers between devices: 231 us -> none  [shards(): lax.all_gather(own_rows.astype(jnp.bfloat16), 'ops', axis=1, tiled=True)]
    pallas_call x0 -> x1, Pallas kernels: none -> 106 us  [shards(): pl.pallas_call(kernel, out_shape=(jax.ShapeDtypeStruct((4, M, M), BF16),...]
    dot_general x5 -> x0, matrix products: 38.6 us -> none  [the longest x2 23.4 us: shards(): contrib = jnp.einsum('tks,ksmq->tmq', routing, terms, precision=highest)]
    psum x1 -> x0, waiting for transfers between devices: 38 us -> none  [broadcast(): return lax.psum(kept, axis)]
  transfers between devices with their start and end apart: 7 -> 0, of which waited for: 7 -> 0; matrix products, arithmetic and copies ran while one was open for 0% -> 0% of each run, Pallas kernels for 0% -> 0%
where the time goes in v2:
time: 113 us
  Pallas kernels  106 us (94%)
  other arithmetic  4.25 us (4%)
  between operations  1.29 us (1%)
    pallas_call x1, Pallas kernels, shards(): pl.pallas_call(kernel, out_shape=(jax.ShapeDtypeStruct((4, M, M), BF16),...  106 us
    mul x1, other arithmetic, shards(): return (wave.astype(F32) * scale, mixed)  4.25 us

profile of v2, /device:TPU:1, one launch (start us, length us, event | category | flops | bytes accessed | tf_op | source)
XLA Modules:
  0.0 112.6 jit_solution(12436029636981651968)
XLA Ops:
  1.3 106.4 %dmrg_window.1 = (bf16[4,512,512]{2,1,0:T(8,128)(2,1)}, bf16[1,512,256]{2,1,0:T(8,128)(2,1)}, f32[1,512]{1,0:T(1,128)}) custom-call(bf16[4,512,512]{2,1,0:T(8,128)(2,1)} %wave.1, bf16[1,512,512]{2,1,0:T(8,128)(2,1)} %left.1, bf16[1,512,512]{2,1,0:T(8,128)(2,1)} %right.1, s32[1]{0:T(128)S(6)} %copy.10.shift, s32[8]{0:T(128)} %sizes.1, s32[2]{0:T(128)} %steps.1, ...), custom_call_target="tpu_custom_call" | custom-call | tf_op jit(solution)/shard_map/dmrg_window/pallas_call | solution.py:445
  107.7 0.0 copy-start
  107.7 4.2 %convert_multiply_fusion = f32[4,512,512]{2,1,0:T(8,128)} fusion(bf16[4,512,512]{2,1,0:T(8,128)(2,1)} %get-tuple-element.5, f32[512]{0:T(512)} %bitcast.1), kind=kLoop, calls=%fused_computation | loop fusion | flops 2097152 | bytes 6293504 | tf_op jit(solution)/shard_map/mul | solution.py:492
  111.9 0.0 copy-done
  111.9 0.7 copy.11
Async XLA Ops:
  107.7 4.3 %copy-start = (bf16[1,512,256]{2,1,0:T(8,128)(2,1)S(1)}, bf16[1,512,256]{2,1,0:T(8,128)(2,1)}, u32[]{:S(2)}) copy-start(bf16[1,512,256]{2,1,0:T(8,128)(2,1)} %get-tuple-element.11) | copy-start | bytes 786436

commit v3 on v2

--- a/solution.py
+++ b/solution.py
@@ -43,9 +43,9 @@
 def kernel(
     wave, left, right, shift, sizes, steps, integ,
     psi_out, mixed_out, scale_out,
-    psi, bas, right_t, near, lmix, chunk, give, acc,
-    csend, cland, s1, l1, l1z, s2, s2z, l2, l2z, nz, nxy, nc, total, rotated,
-    near_s, near_r, c_s, c_r, s1_s, s1_r, s2_s, s2_r, a_s, a_r, b_s, b_r, f_s, f_r, bas_s, bas_r, n_s, n_r,
+    psi, bas, right_t, near, lmix, chunk, acc,
+    shifts, csend, cland, s1, l1, l1z, s2, s2z, l2, l2z, nz, nxy, nc, total, rotated,
+    near_s, near_r, c_s, c_r, s1_s, s1_r, s2_s, s2_r, a_s, a_r, b_s, b_r, f_s, f_r, bas_s, bas_r, n_s, n_r, sh_s, sh_r,
 ):
     ops = lax.axis_index("ops")
     sec = lax.axis_index("sec")
@@ -114,6 +114,7 @@
             block = wave[t, :, 128 * b : 128 * b + 128].astype(F32)
             psi[0, t, b // 2, pl.ds(b % 2 * M, M), :] = jnp.where(ok, block, 0.0).astype(BF16)
 
+    shifts[0, 0] = shift[0]
     loop(0, 4, fill)
     for h in range(2):
         right_t[h] = right[0, 256 * h : 256 * h + 256, :].T
@@ -127,34 +128,32 @@
     def compute(it, s):
         inner = jnp.dot(left[0], columns(psi.at[it, s]), preferred_element_type=F32).astype(BF16)
         theirs = jnp.dot(inner, right_t[1 - core], preferred_element_type=F32).astype(BF16)
-        give[s, pl.ds(0, M), :] = theirs[:, :128]
-        give[s, pl.ds(M, M), :] = theirs[:, 128:]
+        csend[it, s, pl.ds(0, M), :] = theirs[:, :128]
+        csend[it, s, pl.ds(M, M), :] = theirs[:, 128:]
+        if it or s > 1:
+            exchange(it, s)
         mine = jnp.dot(inner, right_t[core], preferred_element_type=F32)
         acc[s, pl.ds(0, M), :] = mine[:, :128]
         acc[s, pl.ds(M, M), :] = mine[:, 128:]
 
-    def source(a, t):
-        s = rem(a * 4 + t - first - shift[0] + 2 * S, S)
+    def source(a, t, by):
+        s = rem(a * 4 + t - first - by + 2 * S, S)
         return jnp.minimum(s, 3), jnp.where(s < 4, 1.0, 0.0).astype(F32)
 
     def core_copy(it, t):
         return copy(csend.at[it, t], cland.at[it, t], c_s.at[it, t], c_r.at[it, t], partner)
 
-    def pick(it, t):
+    def exchange(it, s):
+        start(core_copy(it, s))
+
+    def scatter(it, t):
         for a in range(2):
-            s, gate = source(a, t)
-            for b in range(4):
-                part = pl.ds(256 * b, 256)
-                csend[it, t, a, part, :] = (give[s, part, :].astype(F32) * gate).astype(BF16)
-
-    def scatter(it, t):
-        core_copy(it, t).wait_recv()
-        for a in range(2):
-            s, gate = source(a, t)
+            s, gate = source(a, t, shift[0])
+            ps, pgate = source(a, t, shifts[1, 0])
             for b in range(4):
                 part = pl.ds(256 * b, 256)
                 s1[it, t, a, part, :] = (
-                    acc[s, part, :] * gate + cland[it, t, a, part, :].astype(F32)
+                    acc[s, part, :] * gate + cland[it, ps, part, :].astype(F32) * pgate
                 ).astype(BF16)
         sems = s1_s.at[it, t], s1_r.at[it, t]
         if t == LAST:
@@ -362,23 +361,27 @@
             columns(bas), half, (((0,), (0,)), ((), ())), preferred_element_type=F32
         )
 
+    shift_copy = copy(shifts.at[0], shifts.at[1], sh_s.at[0], sh_r.at[0], partner)
     for s in range(4):
         compute(0, s)
+        if s == 1:
+            pl.semaphore_wait(barrier, 3 + XY - 1 + Z - 1)
+            start(shift_copy)
+            exchange(0, 0)
+            exchange(0, 1)
+    shift_copy.wait_recv()
     for it in range(2):
-        for t in ORDER:
-            pick(it, t)
-            if it == 0 and t == ORDER[0]:
-                pl.semaphore_wait(barrier, 3 + XY - 1 + Z - 1)
-            start(core_copy(it, t))
+        for s in (0, 1, 3, 2):
+            core_copy(it, s).wait_recv()
         for t in ORDER:
             scatter(it, t)
-            if it == 0 and t == LAST:
-                for c in near_copies:
-                    start(c)
         if it == 1:
             mix()
         reduce_first(it, 0)
         reduce_first(it, 3)
+        if it == 0:
+            for c in near_copies:
+                start(c)
         reduce_first(it, 1)
         reduce_second(it, 0)
         reduce_first(it, 2)
@@ -429,6 +432,11 @@
         wait()
 
 
+def finish(wave, mixed, scale, wave_out, mixed_out):
+    wave_out[...] = wave[...].astype(F32) * scale[...]
+    mixed_out[...] = mixed[...]
+
+
 def shards(*args):
     vmem = pl.BlockSpec(memory_space=pltpu.VMEM)
     smem = pl.BlockSpec(memory_space=pltpu.SMEM)
@@ -458,10 +466,10 @@
             low(2, M, M),
             low(M, M),
             full(4, CHUNK, 128),
-            low(4, HALF, 128),
             full(4, HALF, 128),
-            low(2, 4, 2, HALF, 128),
-            low(2, 4, 2, HALF, 128),
+            pltpu.SMEM((2, 1), jnp.int32),
+            low(2, 4, HALF, 128),
+            low(2, 4, HALF, 128),
             low(2, 4, 2, HALF, 128),
             low(2, 3, XY, BLOCK, 128),
             low(2, Z, 2, BLOCK, 128),
@@ -483,13 +491,32 @@
             *pair(2, 4),
             *pair(2),
             *pair(2, 3),
+            *pair(1),
         ],
         compiler_params=pltpu.CompilerParams(
             collective_id=0, has_side_effects=True, vmem_limit_bytes=60 * 2**20
         ),
         name="dmrg_window",
     )(*args)
-    return wave.astype(F32) * scale, mixed
+    steps = 8
+    return pl.pallas_call(
+        finish,
+        grid=(steps,),
+        out_shape=(
+            jax.ShapeDtypeStruct((4, M, M), F32),
+            jax.ShapeDtypeStruct((1, M, M // 2), BF16),
+        ),
+        in_specs=[
+            pl.BlockSpec((1, M // 2, M), lambda i: (i // 2, i % 2, 0)),
+            pl.BlockSpec((1, M // steps, M // 2), lambda i: (0, i, 0)),
+            pl.BlockSpec((1, M), lambda i: (0, 0)),
+        ],
+        out_specs=(
+            pl.BlockSpec((1, M // 2, M), lambda i: (i // 2, i % 2, 0)),
+            pl.BlockSpec((1, M // steps, M // 2), lambda i: (0, i, 0)),
+        ),
+        name="scale_wave",
+    )(wave, mixed, scale)
 
 
 def solution(mesh):

time: 113 us -> 116 us (1.027)
  Pallas kernels: 106 us -> 115 us
  other arithmetic: 4.25 us -> 0 us
    pallas_call x0 -> x1, Pallas kernels: none -> 6.1 us  [shards(): pl.pallas_call(finish, grid=(steps,), out_shape=(jax.ShapeDtypeStruct((4,...]
    mul x1 -> x0, other arithmetic: 4.25 us -> none  [shards(): return (wave.astype(F32) * scale, mixed)]
    pallas_call x1, Pallas kernels: 106 us -> 109 us  [shards(): pl.pallas_call(kernel, out_shape=(jax.ShapeDtypeStruct((4, M, M), BF16),...]
where the time goes in v3:
time: 116 us
  Pallas kernels  115 us (99%)
  between operations  1.28 us (1%)
    pallas_call x1, Pallas kernels, shards(): pl.pallas_call(kernel, out_shape=(jax.ShapeDtypeStruct((4, M, M), BF16),...  109 us
    pallas_call x1, Pallas kernels, shards(): pl.pallas_call(finish, grid=(steps,), out_shape=(jax.ShapeDtypeStruct((4,...  6.1 us

profile of v3, /device:TPU:1, one launch (start us, length us, event | category | flops | bytes accessed | tf_op | source)
XLA Modules:
  0.0 116.2 jit_solution(14065000944514051290)
XLA Ops:
  1.3 108.8 %dmrg_window.1 = (bf16[4,512,512]{2,1,0:T(8,128)(2,1)}, bf16[1,512,256]{2,1,0:T(8,128)(2,1)}, f32[1,512]{1,0:T(1,128)}) custom-call(bf16[4,512,512]{2,1,0:T(8,128)(2,1)} %wave.1, bf16[1,512,512]{2,1,0:T(8,128)(2,1)} %left.1, bf16[1,512,512]{2,1,0:T(8,128)(2,1)} %right.1, s32[1]{0:T(128)S(6)} %copy.9.shift, s32[8]{0:T(128)} %sizes.1, s32[2]{0:T(128)} %steps.1, ...), custom_call_target="tpu_custom_call" | custom-call | tf_op jit(solution)/shard_map/dmrg_window/pallas_call | solution.py:453
  110.1 6.1 %scale_wave.1 = (f32[4,512,512]{2,1,0:T(8,128)}, bf16[1,512,256]{2,1,0:T(8,128)(2,1)}) custom-call(bf16[4,512,512]{2,1,0:T(8,128)(2,1)} %get-tuple-element.5.wave, bf16[1,512,256]{2,1,0:T(8,128)(2,1)} %get-tuple-element.6.mixed, f32[1,512]{1,0:T(1,128)} %get-tuple-element.7.scale), custom_call_target="tpu_custom_call" | custom-call | tf_op jit(solution)/shard_map/scale_wave/pallas_call | solution.py:502

commit v4 on v3

--- a/solution.py
+++ b/solution.py
@@ -41,11 +41,11 @@
 
 
 def kernel(
-    wave, left, right, shift, sizes, steps, integ,
+    wave_hbm, left_hbm, right_hbm, shift_hbm, sizes, steps, integ,
     psi_out, mixed_out, scale_out,
-    psi, bas, right_t, near, lmix, chunk, acc,
+    wave, left, right, shift, psi, bas, right_t, near, lmix, chunk, acc,
     shifts, csend, cland, s1, l1, l1z, s2, s2z, l2, l2z, nz, nxy, nc, total, rotated,
-    near_s, near_r, c_s, c_r, s1_s, s1_r, s2_s, s2_r, a_s, a_r, b_s, b_r, f_s, f_r, bas_s, bas_r, n_s, n_r, sh_s, sh_r,
+    near_s, near_r, c_s, c_r, s1_s, s1_r, s2_s, s2_r, a_s, a_r, b_s, b_r, f_s, f_r, bas_s, bas_r, n_s, n_r, sh_s, sh_r, in_s,
 ):
     ops = lax.axis_index("ops")
     sec = lax.axis_index("sec")
@@ -82,11 +82,22 @@
         sent.append(made.wait_send)
 
     def group(low, high, make, whole, send, recv):
-        loop(low, high, lambda d: make(d).start())
+        if high - low < 8:
+            for d in range(low, high):
+                make(jnp.int32(d)).start()
+        else:
+            loop(low, high, lambda d: make(d).start())
         sent.append(copy(whole, whole, send, recv, partner).wait_send)
 
     def arrived(whole, send, recv):
         copy(whole, whole, send, recv, partner).wait_recv()
+
+    inputs = [pltpu.make_async_copy(wave_hbm.at[t], wave.at[t], in_s.at[t]) for t in range(4)]
+    inputs.append(pltpu.make_async_copy(left_hbm, left, in_s.at[4]))
+    inputs.append(pltpu.make_async_copy(right_hbm, right, in_s.at[5]))
+    inputs.append(pltpu.make_async_copy(shift_hbm, shift, in_s.at[6]))
+    for t in (6, 0, 5, 4, 1, 2, 3):
+        inputs[t].start()
 
     barrier = pltpu.get_barrier_semaphore()
 
@@ -114,13 +125,19 @@
             block = wave[t, :, 128 * b : 128 * b + 128].astype(F32)
             psi[0, t, b // 2, pl.ds(b % 2 * M, M), :] = jnp.where(ok, block, 0.0).astype(BF16)
 
+    inputs[6].wait()
     shifts[0, 0] = shift[0]
-    loop(0, 4, fill)
+    for t in range(4):
+        inputs[t].wait()
+        fill(t)
+    inputs[5].wait()
     for h in range(2):
         right_t[h] = right[0, 256 * h : 256 * h + 256, :].T
     own = [z * G + g if t == LAST else g * Z + z for t in range(4)]
     for t in range(4):
         chunk[t] = psi[0, t, core, rows(own[t], CHUNK), :].astype(F32)
+
+    inputs[4].wait()
 
     def columns(ref):
         return jnp.concatenate([ref[b // 2, pl.ds(b % 2 * M, M), :] for b in range(4)], axis=1)
@@ -375,13 +392,11 @@
             core_copy(it, s).wait_recv()
         for t in ORDER:
             scatter(it, t)
-        if it == 1:
-            mix()
+            if it == 1 and t == LAST:
+                for c in near_copies:
+                    start(c)
         reduce_first(it, 0)
         reduce_first(it, 3)
-        if it == 0:
-            for c in near_copies:
-                start(c)
         reduce_first(it, 1)
         reduce_second(it, 0)
         reduce_first(it, 2)
@@ -390,6 +405,8 @@
         gather_second(it, 0)
         reduce_second(it, 2)
         norm_z(it)
+        if it == 1:
+            mix()
         gather_second(it, 1)
         gather_second(it, 3)
         forward(it, 0)
@@ -432,14 +449,10 @@
         wait()
 
 
-def finish(wave, mixed, scale, wave_out, mixed_out):
-    wave_out[...] = wave[...].astype(F32) * scale[...]
-    mixed_out[...] = mixed[...]
-
-
 def shards(*args):
     vmem = pl.BlockSpec(memory_space=pltpu.VMEM)
     smem = pl.BlockSpec(memory_space=pltpu.SMEM)
+    hbm = pl.BlockSpec(memory_space=pltpu.HBM)
 
     def low(*shape):
         return pltpu.VMEM(shape, BF16)
@@ -457,9 +470,13 @@
             jax.ShapeDtypeStruct((1, M, M // 2), BF16),
             jax.ShapeDtypeStruct((1, M), F32),
         ),
-        in_specs=[vmem, vmem, vmem, smem, smem, smem, smem],
+        in_specs=[hbm, hbm, hbm, hbm, smem, smem, smem],
         out_specs=(vmem, vmem, vmem),
         scratch_shapes=[
+            low(4, M, M),
+            low(1, M, M),
+            low(1, M, M),
+            pltpu.SMEM((1,), jnp.int32),
             low(3, 4, 2, HALF, 128),
             low(2, HALF, 128),
             low(2, M, 256),
@@ -492,31 +509,14 @@
             *pair(2),
             *pair(2, 3),
             *pair(1),
+            pltpu.SemaphoreType.DMA((7,)),
         ],
         compiler_params=pltpu.CompilerParams(
             collective_id=0, has_side_effects=True, vmem_limit_bytes=60 * 2**20
         ),
         name="dmrg_window",
     )(*args)
-    steps = 8
-    return pl.pallas_call(
-        finish,
-        grid=(steps,),
-        out_shape=(
-            jax.ShapeDtypeStruct((4, M, M), F32),
-            jax.ShapeDtypeStruct((1, M, M // 2), BF16),
-        ),
-        in_specs=[
-            pl.BlockSpec((1, M // 2, M), lambda i: (i // 2, i % 2, 0)),
-            pl.BlockSpec((1, M // steps, M // 2), lambda i: (0, i, 0)),
-            pl.BlockSpec((1, M), lambda i: (0, 0)),
-        ],
-        out_specs=(
-            pl.BlockSpec((1, M // 2, M), lambda i: (i // 2, i % 2, 0)),
-            pl.BlockSpec((1, M // steps, M // 2), lambda i: (0, i, 0)),
-        ),
-        name="scale_wave",
-    )(wave, mixed, scale)
+    return wave.astype(F32) * scale, mixed
 
 
 def solution(mesh):

time: 116 us -> 112 us (0.966)
  Pallas kernels: 115 us -> 105 us
  other arithmetic: 0 us -> 4.25 us
    pallas_call x1 -> x0, Pallas kernels: 6.1 us -> none  [shards(): pl.pallas_call(finish, grid=(steps,), out_shape=(jax.ShapeDtypeStruct((4,...]
    mul x0 -> x1, other arithmetic: none -> 4.25 us  [shards(): return (wave.astype(F32) * scale, mixed)]
    pallas_call x1, Pallas kernels: 109 us -> 105 us  [shards(): pl.pallas_call(kernel, out_shape=(jax.ShapeDtypeStruct((4, M, M), BF16),...]
where the time goes in v4:
time: 112 us; the launch traced here: 111 us
  Pallas kernels  105 us (94%)
  other arithmetic  4.25 us (4%)
  between operations  1.29 us (1%)
    pallas_call x1, Pallas kernels, shards(): pl.pallas_call(kernel, out_shape=(jax.ShapeDtypeStruct((4, M, M), BF16),...  105 us
    mul x1, other arithmetic, shards(): return (wave.astype(F32) * scale, mixed)  4.25 us

profile of v4, /device:TPU:1, one launch (start us, length us, event | category | flops | bytes accessed | tf_op | source)
XLA Modules:
  0.0 111.4 jit_solution(7982357776303377494)
XLA Ops:
  1.3 105.2 %dmrg_window.1 = (bf16[4,512,512]{2,1,0:T(8,128)(2,1)}, bf16[1,512,256]{2,1,0:T(8,128)(2,1)}, f32[1,512]{1,0:T(1,128)}) custom-call(bf16[4,512,512]{2,1,0:T(8,128)(2,1)} %wave_hbm.1, bf16[1,512,512]{2,1,0:T(8,128)(2,1)} %left_hbm.1, bf16[1,512,512]{2,1,0:T(8,128)(2,1)} %right_hbm.1, s32[1]{0:T(128)S(6)} %copy.10.shift_hbm, s32[8]{0:T(128)} %sizes.1, ...), custom_call_target="tpu_custom_call" | custom-call | tf_op jit(solution)/shard_map/dmrg_window/pallas_call | solution.py:466
  106.5 0.0 copy-start
  106.5 4.2 %convert_multiply_fusion = f32[4,512,512]{2,1,0:T(8,128)} fusion(bf16[4,512,512]{2,1,0:T(8,128)(2,1)} %get-tuple-element.5, f32[512]{0:T(512)} %bitcast.1), kind=kLoop, calls=%fused_computation | loop fusion | flops 2097152 | bytes 6293504 | tf_op jit(solution)/shard_map/mul | solution.py:519
  110.7 0.0 copy-done
  110.7 0.7 copy.11
Async XLA Ops:
  106.5 4.3 %copy-start = (bf16[1,512,256]{2,1,0:T(8,128)(2,1)S(1)}, bf16[1,512,256]{2,1,0:T(8,128)(2,1)}, u32[]{:S(2)}) copy-start(bf16[1,512,256]{2,1,0:T(8,128)(2,1)} %get-tuple-element.11) | copy-start | bytes 786436

commit v5 on v4

--- a/solution.py
+++ b/solution.py
@@ -21,7 +21,7 @@
 CHUNK = HALF // (G * Z)
 BLOCK = HALF // 8
 LAST = 3
-ORDER = (3, 0, 1, 2)
+ORDER = (0, 3, 1, 2)
 
 
 def loop(low, high, body):
@@ -395,27 +395,33 @@
             if it == 1 and t == LAST:
                 for c in near_copies:
                     start(c)
+        if it == 1:
+            norm_z(0)
         reduce_first(it, 0)
         reduce_first(it, 3)
         reduce_first(it, 1)
+        if it == 1:
+            norm_xy(0)
         reduce_second(it, 0)
         reduce_first(it, 2)
         reduce_second(it, 3)
         reduce_second(it, 1)
         gather_second(it, 0)
         reduce_second(it, 2)
-        norm_z(it)
-        if it == 1:
-            mix()
+        if it == 1:
+            norm_z(1)
         gather_second(it, 1)
         gather_second(it, 3)
+        if it == 1:
+            norm_core(0)
+            mix()
         forward(it, 0)
         if it == 1:
             basis_forward()
+        if it == 1:
+            norm_xy(1)
         gather_second(it, 2)
-        norm_xy(it)
         forward(it, 1)
-        forward(it, 3)
         forward_copy(it, 0).wait_recv()
         if it == 0:
             compute(1, 0)
@@ -427,15 +433,18 @@
             compute(1, 1)
         else:
             write_wave(1)
+        forward(it, 3)
         forward(it, 2)
-        norm_core(it)
+        if it == 1:
+            norm_core(1)
         for t in (3, 2):
             forward_copy(it, t).wait_recv()
             if it == 0:
                 compute(1, t)
             else:
                 write_wave(t)
-        norm_end(it)
+    norm_end(0)
+    norm_end(1)
 
     count = float(S * M * M)
     sum1 = jnp.sum(total[0], axis=(0, 1), keepdims=True)

time: 112 us -> 111 us (level)
  no operation moved by 1% of the time
where the time goes in v5:
time: 111 us
  Pallas kernels  104 us (94%)
  other arithmetic  4.25 us (4%)
  between operations  1.29 us (1%)
    pallas_call x1, Pallas kernels, shards(): pl.pallas_call(kernel, out_shape=(jax.ShapeDtypeStruct((4, M, M), BF16),...  104 us
    mul x1, other arithmetic, shards(): return (wave.astype(F32) * scale, mixed)  4.25 us

profile of v5, /device:TPU:1, one launch (start us, length us, event | category | flops | bytes accessed | tf_op | source)
XLA Modules:
  0.0 110.6 jit_solution(5939656093139850298)
XLA Ops:
  1.3 104.4 %dmrg_window.1 = (bf16[4,512,512]{2,1,0:T(8,128)(2,1)}, bf16[1,512,256]{2,1,0:T(8,128)(2,1)}, f32[1,512]{1,0:T(1,128)}) custom-call(bf16[4,512,512]{2,1,0:T(8,128)(2,1)} %wave_hbm.1, bf16[1,512,512]{2,1,0:T(8,128)(2,1)} %left_hbm.1, bf16[1,512,512]{2,1,0:T(8,128)(2,1)} %right_hbm.1, s32[1]{0:T(128)S(6)} %copy.10.shift_hbm, s32[8]{0:T(128)} %sizes.1, ...), custom_call_target="tpu_custom_call" | custom-call | tf_op jit(solution)/shard_map/dmrg_window/pallas_call | solution.py:475
  105.7 0.0 copy-start
  105.7 4.2 %convert_multiply_fusion = f32[4,512,512]{2,1,0:T(8,128)} fusion(bf16[4,512,512]{2,1,0:T(8,128)(2,1)} %get-tuple-element.5, f32[512]{0:T(512)} %bitcast.1), kind=kLoop, calls=%fused_computation | loop fusion | flops 2097152 | bytes 6293504 | tf_op jit(solution)/shard_map/mul | solution.py:528
  109.9 0.0 copy-done
  109.9 0.7 copy.11
Async XLA Ops:
  105.7 4.3 %copy-start = (bf16[1,512,256]{2,1,0:T(8,128)(2,1)S(1)}, bf16[1,512,256]{2,1,0:T(8,128)(2,1)}, u32[]{:S(2)}) copy-start(bf16[1,512,256]{2,1,0:T(8,128)(2,1)} %get-tuple-element.11) | copy-start | bytes 786436

commit v6 on v5

--- a/solution.py
+++ b/solution.py
@@ -42,10 +42,10 @@
 
 def kernel(
     wave_hbm, left_hbm, right_hbm, shift_hbm, sizes, steps, integ,
-    psi_out, mixed_out, scale_out,
-    wave, left, right, shift, psi, bas, right_t, near, lmix, chunk, acc,
+    psi_hbm, mixed_out, scale_out,
+    wave, left, right, shift, psi_out, psi, bas, right_t, near, lmix, chunk, acc,
     shifts, csend, cland, s1, l1, l1z, s2, s2z, l2, l2z, nz, nxy, nc, total, rotated,
-    near_s, near_r, c_s, c_r, s1_s, s1_r, s2_s, s2_r, a_s, a_r, b_s, b_r, f_s, f_r, bas_s, bas_r, n_s, n_r, sh_s, sh_r, in_s,
+    near_s, near_r, c_s, c_r, s1_s, s1_r, s2_s, s2_r, a_s, a_r, b_s, b_r, f_s, f_r, bas_s, bas_r, n_s, n_r, sh_s, sh_r, in_s, out_s,
 ):
     ops = lax.axis_index("ops")
     sec = lax.axis_index("sec")
@@ -348,6 +348,9 @@
     def write_wave(t):
         for b in range(4):
             psi_out[t, :, 128 * b : 128 * b + 128] = psi[2, t, b // 2, pl.ds(b % 2 * M, M), :]
+        made = pltpu.make_async_copy(psi_out.at[t], psi_hbm.at[t], out_s.at[t])
+        made.start()
+        sent.append(made.wait)
 
     bas_copy = copy(bas.at[core], bas.at[core], bas_s.at[1], bas_r.at[1], partner)
 
@@ -480,12 +483,13 @@
             jax.ShapeDtypeStruct((1, M), F32),
         ),
         in_specs=[hbm, hbm, hbm, hbm, smem, smem, smem],
-        out_specs=(vmem, vmem, vmem),
+        out_specs=(hbm, vmem, vmem),
         scratch_shapes=[
             low(4, M, M),
             low(1, M, M),
             low(1, M, M),
             pltpu.SMEM((1,), jnp.int32),
+            low(4, M, M),
             low(3, 4, 2, HALF, 128),
             low(2, HALF, 128),
             low(2, M, 256),
@@ -519,6 +523,7 @@
             *pair(2, 3),
             *pair(1),
             pltpu.SemaphoreType.DMA((7,)),
+            pltpu.SemaphoreType.DMA((4,)),
         ],
         compiler_params=pltpu.CompilerParams(
             collective_id=0, has_side_effects=True, vmem_limit_bytes=60 * 2**20

time: 111 us -> 111 us (level)
  no operation moved by 1% of the time
where the time goes in v6:
time: 111 us
  Pallas kernels  104 us (94%)
  other arithmetic  4.25 us (4%)
  between operations  1.29 us (1%)
    pallas_call x1, Pallas kernels, shards(): pl.pallas_call(kernel, out_shape=(jax.ShapeDtypeStruct((4, M, M), BF16),...  104 us
    mul x1, other arithmetic, shards(): return (wave.astype(F32) * scale, mixed)  4.25 us

profile of v6, /device:TPU:1, one launch (start us, length us, event | category | flops | bytes accessed | tf_op | source)
XLA Modules:
  0.0 110.5 jit_solution(14300739853244789145)
XLA Ops:
  1.3 104.3 %dmrg_window.1 = (bf16[4,512,512]{2,1,0:T(8,128)(2,1)}, bf16[1,512,256]{2,1,0:T(8,128)(2,1)}, f32[1,512]{1,0:T(1,128)}) custom-call(bf16[4,512,512]{2,1,0:T(8,128)(2,1)} %wave_hbm.1, bf16[1,512,512]{2,1,0:T(8,128)(2,1)} %left_hbm.1, bf16[1,512,512]{2,1,0:T(8,128)(2,1)} %right_hbm.1, s32[1]{0:T(128)S(6)} %copy.10.shift_hbm, s32[8]{0:T(128)} %sizes.1, ...), custom_call_target="tpu_custom_call" | custom-call | tf_op jit(solution)/shard_map/dmrg_window/pallas_call | solution.py:478
  105.6 0.0 copy-start
  105.6 4.2 %convert_multiply_fusion = f32[4,512,512]{2,1,0:T(8,128)} fusion(bf16[4,512,512]{2,1,0:T(8,128)(2,1)} %get-tuple-element.5, f32[512]{0:T(512)} %bitcast.1), kind=kLoop, calls=%fused_computation | loop fusion | flops 2097152 | bytes 6293504 | tf_op jit(solution)/shard_map/mul | solution.py:533
  109.8 0.0 copy-done
  109.8 0.7 copy.11
Async XLA Ops:
  105.6 4.3 %copy-start = (bf16[1,512,256]{2,1,0:T(8,128)(2,1)S(1)}, bf16[1,512,256]{2,1,0:T(8,128)(2,1)}, u32[]{:S(2)}) copy-start(bf16[1,512,256]{2,1,0:T(8,128)(2,1)} %get-tuple-element.11) | copy-start | bytes 786436

commit v7 on v5

--- a/solution.py
+++ b/solution.py
@@ -82,7 +82,7 @@
         sent.append(made.wait_send)
 
     def group(low, high, make, whole, send, recv):
-        if high - low < 8:
+        if high - low < XY:
             for d in range(low, high):
                 make(jnp.int32(d)).start()
         else:

time: 111 us -> 111 us (level)
  no operation moved by 1% of the time
where the time goes in v7:
time: 111 us
  Pallas kernels  105 us (95%)
  other arithmetic  4.25 us (4%)
  between operations  1.29 us (1%)
    pallas_call x1, Pallas kernels, shards(): pl.pallas_call(kernel, out_shape=(jax.ShapeDtypeStruct((4, M, M), BF16),...  105 us
    mul x1, other arithmetic, shards(): return (wave.astype(F32) * scale, mixed)  4.25 us

profile of v7, /device:TPU:1, one launch (start us, length us, event | category | flops | bytes accessed | tf_op | source)
XLA Modules:
  0.0 110.8 jit_solution(12335653080796204058)
XLA Ops:
  1.3 104.6 %dmrg_window.1 = (bf16[4,512,512]{2,1,0:T(8,128)(2,1)}, bf16[1,512,256]{2,1,0:T(8,128)(2,1)}, f32[1,512]{1,0:T(1,128)}) custom-call(bf16[4,512,512]{2,1,0:T(8,128)(2,1)} %wave_hbm.1, bf16[1,512,512]{2,1,0:T(8,128)(2,1)} %left_hbm.1, bf16[1,512,512]{2,1,0:T(8,128)(2,1)} %right_hbm.1, s32[1]{0:T(128)S(6)} %copy.10.shift_hbm, s32[8]{0:T(128)} %sizes.1, ...), custom_call_target="tpu_custom_call" | custom-call | tf_op jit(solution)/shard_map/dmrg_window/pallas_call | solution.py:475
  105.9 0.0 copy-start
  105.9 4.2 %convert_multiply_fusion = f32[4,512,512]{2,1,0:T(8,128)} fusion(bf16[4,512,512]{2,1,0:T(8,128)(2,1)} %get-tuple-element.5, f32[512]{0:T(512)} %bitcast.1), kind=kLoop, calls=%fused_computation | loop fusion | flops 2097152 | bytes 6293504 | tf_op jit(solution)/shard_map/mul | solution.py:528
  110.1 0.0 copy-done
  110.1 0.7 copy.11
Async XLA Ops:
  105.9 4.3 %copy-start = (bf16[1,512,256]{2,1,0:T(8,128)(2,1)S(1)}, bf16[1,512,256]{2,1,0:T(8,128)(2,1)}, u32[]{:S(2)}) copy-start(bf16[1,512,256]{2,1,0:T(8,128)(2,1)} %get-tuple-element.11) | copy-start | bytes 786436
